TPU v7x, 32 devices: a whole 2x2x4 slice. The times are simulated.
32 devices in a mesh: wide: 8 (over y, x, core), narrow: 4 (over z).
Axes of the slice: x: 2, y: 2, z: 4, core: 2. Of those that a mesh axis runs over, the one named last changes fastest.
Arguments:
- hidden: bfloat16 [96, 512, 768], P(('wide', 'narrow')), may hold values from -6 to 6
- lengths: int32 [96], P(('wide', 'narrow')), may hold values from 16 to 512, as said below
- slot_order: int32 [96], P(('wide', 'narrow')), may hold values from 0 to 2, as said below
- labels: int32 [96], P(('wide', 'narrow')), may hold values from -1 to 2, as said below
- w_qkv: bfloat16 [2, 768, 2304], replicated, may hold values from -0.21875 to 0.21875
- b_query: float32 [2, 768], replicated, may hold values from -3 to 3
- b_value: float32 [2, 768], replicated, may hold values from -3 to 3
- w_out: bfloat16 [2, 768, 768], replicated, may hold values from -0.625 to 0.625
- b_out: float32 [2, 768], replicated, may hold values from -3 to 3
- ln1_gain: float32 [2, 768], replicated, may hold values from 0.1 to 1.9
- ln1_bias: float32 [2, 768], replicated, may hold values from -3 to 3
- w_in: bfloat16 [2, 768, 3072], replicated, may hold values from -0.21875 to 0.21875
- b_in: float32 [2, 3072], replicated, may hold values from -3 to 3
- w_back: bfloat16 [2, 3072, 768], replicated, may hold values from -0.15625 to 0.15625
- b_back: float32 [2, 768], replicated, may hold values from -3 to 3
- ln2_gain: float32 [2, 768], replicated, may hold values from 0.1 to 1.9
- ln2_bias: float32 [2, 768], replicated, may hold values from -3 to 3
- pool_w: float32 [2, 768, 768], replicated, may hold values from -0.21875 to 0.21875
- pool_b: float32 [2, 768], replicated, may hold values from -3 to 3
- cls_w: float32 [2, 768, 3], replicated, may hold values from -0.625 to 0.625
- cls_b: float32 [2, 3], replicated, may hold values from -3 to 3
Outputs:
- block_states: bfloat16 [2, 96, 512, 768], P(None, ('wide', 'narrow'))
- logits: float32 [2, 96, 3], P(None, ('wide', 'narrow'))
- losses: float32 [2], replicated
- grad_pool_w: float32 [2, 768, 768], replicated
- grad_pool_b: float32 [2, 768], replicated
- grad_cls_w: float32 [2, 768, 3], replicated
- grad_cls_b: float32 [2, 3], replicated
- first_grads: float32 [2, 96, 768], P(None, ('wide', 'narrow'))
Inputs may be any that keep to these rules, and one draw needn't show every extreme that they name: `lengths`: sequence 0 has length 512; the last sequence has length 16. `slot_order`: within each device's 3 slots every local index appears once. `labels`: the first arriving sequence of each device carries a label.
All inputs are finite; a program needn't handle non-finite values.
Results may differ from a plain program's by a relative error of at most 0.0085.
Values sent between devices are 32-bit elements; how exact they have to be, the bound alone decides.
A program may use at most 256 MiB of HBM per device.

v0:
```python
import functools
import math

import jax
import jax.numpy as jnp
from jax import lax
from jax.experimental import pallas as pl
from jax.experimental.pallas import tpu as pltpu
from jax.sharding import PartitionSpec as P

HEAD = 64
LEAD = 128
MESH = pl.DeviceIdType.MESH
epsilon = 1e-12
bf16 = jnp.bfloat16
f32 = jnp.float32
SCALE = HEAD**-0.5 * math.log2(math.e)
SUM_LOW = 2.0**-60
SUM_HIGH = 2.0**100


def split(values):
    high = values.astype(bf16)
    return high, (values - high.astype(f32)).astype(bf16)


def gelu(values):
    return (0.5 * values) * (1.0 + lax.erf(values * math.sqrt(0.5)))


def norm_rows(values, gain, shift):
    center = values - jnp.mean(values, -1, keepdims=True)
    spread = jnp.mean(center * center, -1, keepdims=True)
    return center * lax.rsqrt(spread + epsilon) * gain + shift


def blocks_kernel(
    order,
    lens,
    labels,
    hidden,
    w_qkv,
    w_out,
    w_in,
    w_back,
    b_query,
    b_value,
    b_out,
    ln1_gain,
    ln1_bias,
    b_in,
    b_back,
    ln2_gain,
    ln2_bias,
    states,
    context,
    packet,
    x_buf,
    last_buf,
    qkv_buf,
    out_buf,
    in_buf,
    back_buf,
    turned,
    columns,
    q_buf,
    k_buf,
    v_buf,
    p_buf,
    ct_buf,
    c_buf,
    m_buf,
    mb_buf,
    y_buf,
    h_buf,
    fine,
    vec_bufs,
    packet_buf,
    order_buf,
    lens_buf,
    labels_buf,
    w_sem,
    x_sem,
    o_sem,
    c_sem,
    v_sem,
):
    depth, width = b_query.shape
    slots, length = x_buf.shape[1:3]
    heads = width // HEAD
    hidden_units = b_in.shape[1]
    lead = last_buf.shape[0] // slots
    tile = length // 2
    spans = [slice(t * tile, (t + 1) * tile) for t in range(2)]

    def fetch_x(s):
        return pltpu.make_async_copy(hidden.at[order[s]], x_buf.at[0, s], x_sem.at[s])

    def fetch_qkv(l, part):
        cols = pl.ds(part * width, width)
        return pltpu.make_async_copy(
            w_qkv.at[l, :, cols], qkv_buf.at[l, :, cols], w_sem.at[l, part]
        )

    def fetch_rest(l, number):
        source = (w_out, w_in, w_back)[number]
        target = (out_buf, in_buf, back_buf)[number]
        return pltpu.make_async_copy(source.at[l], target.at[l], w_sem.at[l, 3 + number])

    def put_states(l, s):
        return pltpu.make_async_copy(x_buf.at[l + 1, s], states.at[l, s], o_sem.at[l, s])

    def put_last(s):
        return pltpu.make_async_copy(
            last_buf.at[pl.ds(s * lead, lead)],
            states.at[depth - 1, s, pl.ds(0, lead)],
            o_sem.at[depth - 1, s],
        )

    def put_context(s):
        rows = pl.ds(lead, length - lead)
        return pltpu.make_async_copy(c_buf.at[s, rows], context.at[s, rows], c_sem.at[s])

    vectors = (b_query, b_value, b_out, ln1_gain, ln1_bias, b_in, b_back, ln2_gain, ln2_bias)
    scalars = ((order, order_buf), (lens, lens_buf), (labels, labels_buf))
    small = [
        pltpu.make_async_copy(source, target, v_sem.at[number])
        for number, (source, target) in enumerate((*scalars, *zip(vectors, vec_bufs)))
    ]
    put_packet = pltpu.make_async_copy(packet_buf, packet, v_sem.at[0])
    order, lens, labels = order_buf, lens_buf, labels_buf
    b_query, b_value, b_out, ln1_gain, ln1_bias, b_in, b_back, ln2_gain, ln2_bias = vec_bufs
    for copy in small[:5]:
        copy.start()
    fetch_qkv(0, 0).start()
    fetch_qkv(0, 2).start()
    fetch_qkv(0, 1).start()
    for copy in small[5:]:
        copy.start()
    q_buf[...] = jnp.zeros_like(q_buf)
    small[0].wait()
    for number in range(slots):
        fetch_x(number).start()
    for copy in small[1:]:
        copy.wait()

    for l in range(depth):
        for number, bias in enumerate((b_query, b_value)):
            for j in range(width // 128):
                offset = number * width + j * 128
                columns[l, offset : offset + 128] = jnp.broadcast_to(
                    bias[l : l + 1, j * 128 : (j + 1) * 128], (128, 128)
                ).T

    def turn(l, block):
        skip = jnp.where(block >= width // 128, width, 0)
        lanes = pl.ds(pl.multiple_of(block * 128 + skip, 128), 128)
        rows = pl.ds(pl.multiple_of(block * 128, 128), 128)
        turned[rows] = qkv_buf[l, :, lanes].T

    def project(l, s, keys):
        rows = x_buf[l, s]
        some = rows[:keys]
        k_buf[:keys] = jnp.dot(
            some, qkv_buf[l, :, width : 2 * width], preferred_element_type=f32
        ).astype(bf16)
        seen = (
            lax.broadcasted_iota(jnp.int32, (HEAD, keys), 1) < lens[order[s]]
        ).astype(f32)
        queries = lax.dot_general(
            turned[:width], rows, (((1,), (1,)), ((), ())), preferred_element_type=f32
        )
        values = lax.dot_general(
            turned[width:], some, (((1,), (1,)), ((), ())), preferred_element_type=f32
        )
        for h in range(heads):
            at = slice(h * HEAD, (h + 1) * HEAD)
            half = slice((h % 2) * HEAD, (h % 2 + 1) * HEAD)
            q_buf[h, half] = (
                queries[at] + jnp.tile(columns[l, at, :], (1, length // 128))
            ).astype(bf16)
            av = slice(width + h * HEAD, width + (h + 1) * HEAD)
            v_buf[h, :HEAD, :keys] = (
                (values[at] + jnp.tile(columns[l, av, :], (1, keys // 128))) * seen
            ).astype(bf16)
            v_buf[h, HEAD:, :keys] = seen.astype(bf16)

    def attend(s, keys):
        def score(h):
            pair = slice((h // 2) * 128, (h // 2 + 1) * 128)
            scores = jnp.dot(k_buf[:keys, pair], q_buf[h], preferred_element_type=f32)
            p_buf[h % 4, :keys] = jnp.exp2(scores * SCALE).astype(bf16)

        def mix(h):
            both = jnp.dot(
                v_buf[h, :, :keys], p_buf[h % 4, :keys], preferred_element_type=f32
            )
            sums = both[HEAD:]
            good = (sums[:8] >= SUM_LOW) & (sums[:8] <= SUM_HIGH)
            fine[...] = jnp.where(good, fine[...], 0.0)
            half = slice((h % 2) * HEAD, (h % 2 + 1) * HEAD)
            ct_buf[(h // 2) % 2, half] = (both[:HEAD] * (1.0 / sums)).astype(bf16)
            if h % 2 == 1:
                pair = slice((h // 2) * 128, (h // 2 + 1) * 128)
                c_buf[s, :, pair] = ct_buf[(h // 2) % 2].T

        score(0)
        for h in range(heads):
            if h + 1 < heads:
                score(h + 1)
            mix(h)

    def attend_shifted(s):
        count = lens[order[s]]

        def pair_step(number, carry):
            lanes = pl.ds(pl.multiple_of(number * 128, 128), 128)
            for side in range(2):
                h = number * 2 + side
                scores = (
                    jnp.dot(k_buf[:, lanes], q_buf[h], preferred_element_type=f32) * SCALE
                )
                seen = lax.broadcasted_iota(jnp.int32, scores.shape, 0) < count
                scores = jnp.where(seen, scores, -1e30)
                highest = jnp.max(scores, 0, keepdims=True)
                p_buf[side] = jnp.exp2(scores - highest).astype(bf16)
                both = jnp.dot(v_buf[h], p_buf[side], preferred_element_type=f32)
                ct_buf[0, side * HEAD : (side + 1) * HEAD] = (
                    both[:HEAD] / both[HEAD:]
                ).astype(bf16)
            c_buf[s, :, lanes] = ct_buf[0].T
            return carry

        lax.fori_loop(0, heads // 2, pair_step, 0)

    def front(l):
        fine[...] = jnp.ones_like(fine)

        def step(s, carry):
            @pl.when(l == 0)
            def _():
                fetch_x(s).wait()

            tiles = (lens[order[s]] + 127) // 128
            for number in range(2, length // 128 + 1):
                here = (tiles <= number) if number == 2 else (tiles == number)

                @pl.when(here)
                def _(number=number):
                    project(l, s, number * 128)
                    attend(s, number * 128)

            return carry

        lax.fori_loop(0, slots, step, 0)

        @pl.when(jnp.min(fine[...]) < 0.5)
        def _():
            def again(s, carry):
                project(l, s, length)
                attend_shifted(s)
                return carry

            lax.fori_loop(0, slots, again, 0)

    def join(l, slot, contexts, inputs):
        attended = jnp.dot(contexts, out_buf[l], preferred_element_type=f32)
        values = inputs.astype(f32) + (attended + b_out[l : l + 1])
        middle = norm_rows(values, ln1_gain[l : l + 1], ln1_bias[l : l + 1])
        size = middle.shape[0]
        m_buf[slot, :size] = middle
        mb_buf[slot, :size] = middle.astype(bf16)

    def expand(l, slot, size=tile):
        chunk = 512
        for j in range(hidden_units // chunk):
            units = slice(j * chunk, (j + 1) * chunk)
            inner = jnp.dot(mb_buf[slot, :size], in_buf[l, :, units], preferred_element_type=f32)
            h_buf[slot, :size, units] = gelu(inner + b_in[l : l + 1, units]).astype(bf16)

    def contract(l, slot, size=tile):
        back = jnp.dot(h_buf[slot, :size], back_buf[l], preferred_element_type=f32)
        y_buf[slot, :size] = m_buf[slot, :size] + back + b_back[l : l + 1]

    def settle(l, slot, size=tile):
        return norm_rows(y_buf[slot, :size], ln2_gain[l : l + 1], ln2_bias[l : l + 1]).astype(bf16)

    def rear(l):
        def enter(s, half):
            join(l, half, c_buf[s, spans[half]], x_buf[l, s, spans[half]])

        enter(0, 0)

        def step(s, carry):
            x_buf[l + 1, jnp.maximum(s - 1, 0), spans[1]] = settle(l, 1)
            expand(l, 0)
            enter(s, 1)
            contract(l, 0)
            x_buf[l + 1, s, spans[0]] = settle(l, 0)
            expand(l, 1)
            enter(jnp.minimum(s + 1, slots - 1), 0)
            contract(l, 1)
            blocks = 2 * width // 128 // slots
            for number in range(blocks):
                turn(l + 1, s * blocks + number)

            @pl.when(s > 0)
            def _():
                put_states(l, s - 1).start()

            return carry

        lax.fori_loop(0, slots, step, 0)
        x_buf[l + 1, slots - 1, spans[1]] = settle(l, 1)
        put_states(l, slots - 1).start()

    def rear_lead(l):
        half = slots * lead // 2
        contexts = jnp.concatenate([c_buf[s, :lead] for s in range(slots)])
        inputs = jnp.concatenate([x_buf[l, s, :lead] for s in range(slots)])
        for t in range(2):
            rows = slice(t * half, (t + 1) * half)
            join(l, t, contexts[rows], inputs[rows])
        for t in range(2):
            expand(l, t, half)
        for t in range(2):
            contract(l, t, half)
        for t in range(2):
            last_buf[t * half : (t + 1) * half] = settle(l, t, half)
        for s in range(slots):
            put_last(s).start()

    for part in (0, 2):
        fetch_qkv(0, part).wait()
        for j in range(width // 128):
            turn(0, part // 2 * (width // 128) + j)
    fetch_qkv(0, 1).wait()

    def layer(l, carry):
        for number in range(3):
            fetch_rest(l, number).start()

        @pl.when(l < depth - 1)
        def _():
            for part in range(3):
                fetch_qkv(l + 1, part).start()

        front(l)

        @pl.when(l == depth - 1)
        def _():
            for s in range(slots):
                put_context(s).start()

        for number in range(3):
            fetch_rest(l, number).wait()

        for k in range(depth - 1):

            @pl.when(l == k)
            def _(k=k):
                for part in range(3):
                    fetch_qkv(k + 1, part).wait()
                rear(k)

        return carry

    lax.fori_loop(0, depth, layer, 0)
    rear_lead(depth - 1)
    lane = lax.broadcasted_iota(jnp.int32, packet.shape, 1)
    place = lax.broadcasted_iota(jnp.int32, packet.shape, 0)
    marks = jnp.zeros(packet.shape, f32)
    for s in range(slots):
        marks = jnp.where(lane == s, labels[order[s]].astype(f32), marks)
    packet_buf[...] = jnp.where(place == slots, marks, 0.0)
    for l in range(depth):
        for s in range(slots):
            row = l * (slots + 1) + s
            if l < depth - 1:
                packet_buf[row : row + 1] = x_buf[l + 1, s, 0:1].astype(f32)
            else:
                packet_buf[row : row + 1] = last_buf[s * lead : s * lead + 1].astype(f32)
    put_packet.start()
    for s in range(slots):
        for l in range(depth - 1):
            put_states(l, s).wait()
        put_last(s).wait()
        put_context(s).wait()
    put_packet.wait()


def run_blocks(hidden, lengths, slot_order, labels, stacks):
    (
        w_qkv,
        b_query,
        b_value,
        w_out,
        b_out,
        ln1_gain,
        ln1_bias,
        w_in,
        b_in,
        w_back,
        b_back,
        ln2_gain,
        ln2_bias,
    ) = stacks
    slots, length, width = hidden.shape
    depth = w_qkv.shape[0]
    units = w_in.shape[2]
    heads = width // HEAD
    tile = length // 2
    vectors = (b_query, b_value, b_out, ln1_gain, ln1_bias, b_in, b_back, ln2_gain, ln2_bias)
    place_hbm = pl.BlockSpec(memory_space=pl.ANY)
    return pl.pallas_call(
        blocks_kernel,
        name="blocks",
        out_shape=(
            jax.ShapeDtypeStruct((depth, slots, length, width), bf16),
            jax.ShapeDtypeStruct((slots, length, width), bf16),
            jax.ShapeDtypeStruct((depth * (slots + 1), width), f32),
        ),
        in_specs=[place_hbm] * 17,
        out_specs=(place_hbm,) * 3,
        scratch_shapes=[
            pltpu.VMEM((depth, slots, length, width), bf16),
            pltpu.VMEM((slots * LEAD, width), bf16),
            pltpu.VMEM((depth, width, 3 * width), bf16),
            pltpu.VMEM((depth, width, width), bf16),
            pltpu.VMEM((depth, width, units), bf16),
            pltpu.VMEM((depth, units, width), bf16),
            pltpu.VMEM((2 * width, width), bf16),
            pltpu.VMEM((depth, 2 * width, 128), f32),
            pltpu.VMEM((heads, 2 * HEAD, length), bf16),
            pltpu.VMEM((length, width), bf16),
            pltpu.VMEM((heads, 2 * HEAD, length), bf16),
            pltpu.VMEM((4, length, length), bf16),
            pltpu.VMEM((2, 2 * HEAD, length), bf16),
            pltpu.VMEM((slots, length, width), bf16),
            pltpu.VMEM((2, tile, width), f32),
            pltpu.VMEM((2, tile, width), bf16),
            pltpu.VMEM((2, tile, width), f32),
            pltpu.VMEM((2, tile, units), bf16),
            pltpu.VMEM((8, length), f32),
            [pltpu.VMEM(vector.shape, f32) for vector in vectors],
            pltpu.VMEM((depth * (slots + 1), width), f32),
            pltpu.SMEM((slots,), jnp.int32),
            pltpu.SMEM((slots,), jnp.int32),
            pltpu.SMEM((slots,), jnp.int32),
            pltpu.SemaphoreType.DMA((depth, 6)),
            pltpu.SemaphoreType.DMA((slots,)),
            pltpu.SemaphoreType.DMA((depth, slots)),
            pltpu.SemaphoreType.DMA((slots,)),
            pltpu.SemaphoreType.DMA((3 + len(vectors),)),
        ],
        compiler_params=pltpu.CompilerParams(vmem_limit_bytes=62 * 1024 * 1024),
    )(
        slot_order,
        lengths,
        labels,
        hidden,
        w_qkv,
        w_out,
        w_in,
        w_back,
        *vectors,
    )


def finish_kernel(
    packet,
    states,
    context,
    w_out,
    w_in,
    w_back,
    b_out,
    ln1_gain,
    ln1_bias,
    b_in,
    b_back,
    ln2_gain,
    ln2_bias,
    gathered,
    rest,
    x_buf,
    c_buf,
    out_buf,
    in_buf,
    back_buf,
    m_buf,
    mb_buf,
    h_buf,
    vec_bufs,
    t_sem,
    w_sem,
    o_sem,
    v_sem,
    keep_sem,
    near_send,
    near_recv,
    far_send,
    far_recv,
    twin_send,
    twin_recv,
):
    groups, lines = gathered.shape[:2]
    group, line = lax.axis_index("wide"), lax.axis_index("narrow")
    depth, slots = states.shape[:2]
    rows, width = x_buf.shape[1:]
    hidden_units = b_in.shape[1]
    chunk = 512
    chunks = hidden_units // chunk
    l = depth - 1
    lead = pl.ds(LEAD, rows)

    def near(step):
        return (group, lax.rem(line + step, lines))

    side = lax.rem(group, 2)

    def far(step):
        return (lax.rem(group + 2 * step, groups), line)

    twin = (group + 1 - 2 * side, line)

    def near_copy(step):
        return pltpu.make_async_remote_copy(
            src_ref=packet,
            dst_ref=gathered.at[group, line],
            send_sem=near_send,
            recv_sem=near_recv,
            device_id=near(step),
            device_id_type=MESH,
        )

    def far_copy(step):
        return pltpu.make_async_remote_copy(
            src_ref=gathered.at[group],
            dst_ref=gathered.at[group],
            send_sem=far_send,
            recv_sem=far_recv,
            device_id=far(step),
            device_id_type=MESH,
        )

    def near_all():
        return pltpu.make_async_remote_copy(
            src_ref=gathered.at[0, pl.ds(0, lines - 1)],
            dst_ref=gathered.at[0, pl.ds(0, lines - 1)],
            send_sem=near_send,
            recv_sem=near_recv,
            device_id=near(1),
            device_id_type=MESH,
        )

    def far_all():
        return pltpu.make_async_remote_copy(
            src_ref=gathered.at[pl.ds(0, groups // 2 - 1)],
            dst_ref=gathered.at[pl.ds(0, groups // 2 - 1)],
            send_sem=far_send,
            recv_sem=far_recv,
            device_id=far(1),
            device_id_type=MESH,
        )

    def twin_copy(step):
        return pltpu.make_async_remote_copy(
            src_ref=gathered.at[2 * step + side],
            dst_ref=gathered.at[2 * step + side],
            send_sem=twin_send,
            recv_sem=twin_recv,
            device_id=twin,
            device_id_type=MESH,
        )

    def twin_all():
        return pltpu.make_async_remote_copy(
            src_ref=gathered.at[pl.ds(0, groups // 2)],
            dst_ref=gathered.at[pl.ds(0, groups // 2)],
            send_sem=twin_send,
            recv_sem=twin_recv,
            device_id=twin,
            device_id_type=MESH,
        )

    def keep_own():
        return pltpu.make_async_copy(packet, gathered.at[group, line], keep_sem)

    def begin(copy):
        def body(step, carry):
            copy(step).start()
            return carry

        return body

    def greet(place):
        def body(step, carry):
            pl.semaphore_signal(barrier, inc=1, device_id=place(step), device_id_type=MESH)
            return carry

        return body

    def fetch_tile(s):
        return (
            pltpu.make_async_copy(context.at[s, lead], c_buf.at[s], t_sem.at[0, s]),
            pltpu.make_async_copy(states.at[l - 1, s, lead], x_buf.at[s], t_sem.at[1, s]),
        )

    def fetch_out():
        return pltpu.make_async_copy(w_out.at[l], out_buf, w_sem.at[0])

    def fetch_in(j):
        units = pl.ds(j * chunk, chunk)
        return pltpu.make_async_copy(
            w_in.at[l, :, units], in_buf.at[:, units], w_sem.at[1 + j]
        )

    def fetch_back(j):
        units = pl.ds(j * chunk, chunk)
        return pltpu.make_async_copy(
            w_back.at[l, units], back_buf.at[units], w_sem.at[1 + chunks + j]
        )

    def put_rest(s):
        return pltpu.make_async_copy(x_buf.at[s], rest.at[s], o_sem.at[s])

    barrier = pltpu.get_barrier_semaphore()
    lax.fori_loop(1, lines, greet(near), 0)
    lax.fori_loop(1, groups // 2, greet(far), 0)
    pl.semaphore_signal(barrier, inc=1, device_id=twin, device_id_type=MESH)
    vectors = (b_out, ln1_gain, ln1_bias, b_in, b_back, ln2_gain, ln2_bias)
    small = [
        pltpu.make_async_copy(source, target, v_sem.at[number])
        for number, (source, target) in enumerate(zip(vectors, vec_bufs))
    ]
    b_out, ln1_gain, ln1_bias, b_in, b_back, ln2_gain, ln2_bias = vec_bufs
    queue = [*fetch_tile(0), fetch_out()]
    for j in range(chunks):
        queue.append(fetch_in(j))
        if 0 < j < slots:
            queue += fetch_tile(j)
    queue += [fetch_back(j) for j in range(chunks)]
    queue.reverse()

    def advance(number):
        for _ in range(min(number, len(queue))):
            queue.pop().start()

    for copy in small:
        copy.start()
    advance(3)
    pl.semaphore_wait(barrier, lines + groups // 2 - 1)
    lax.fori_loop(1, lines, begin(near_copy), 0)
    keep_own().start()
    for copy in small:
        copy.wait()
    advance(4)

    def join(s):
        attended = jnp.dot(c_buf[s], out_buf[...], preferred_element_type=f32)
        m_buf[s] = x_buf[s].astype(f32) + (attended + b_out[l : l + 1])

    def norm_first(s, span):
        middle = norm_rows(m_buf[s, span], ln1_gain[l : l + 1], ln1_bias[l : l + 1])
        m_buf[s, span] = middle
        mb_buf[s, span] = middle.astype(bf16)

    def expand(s, j):
        units = slice(j * chunk, (j + 1) * chunk)
        inner = jnp.dot(mb_buf[s], in_buf[:, units], preferred_element_type=f32)
        h_buf[s, :, units] = gelu(inner + b_in[l : l + 1, units]).astype(bf16)

    def contract(s, span):
        back = jnp.dot(h_buf[s, span], back_buf[...], preferred_element_type=f32)
        m_buf[s, span] = m_buf[s, span] + back + b_back[l : l + 1]

    def settle(s, span):
        x_buf[s, span] = norm_rows(
            m_buf[s, span], ln2_gain[l : l + 1], ln2_bias[l : l + 1]
        ).astype(bf16)

    def cut(parts):
        size = rows // parts
        return [slice(t * size, (t + 1) * size) for t in range(parts)]

    for copy in fetch_tile(0):
        copy.wait()
    fetch_out().wait()
    advance(3)
    join(0)
    for span in cut(2):
        norm_first(0, span)
    for s in range(slots):
        if s + 1 < slots:
            for copy in fetch_tile(s + 1):
                copy.wait()
        for j, span in enumerate(cut(chunks)):
            if s == 0:
                fetch_in(j).wait()
                advance(2)
            expand(s, j)
            if j == 0 and s + 1 < slots:
                join(s + 1)
            if s + 1 < slots:
                norm_first(s + 1, span)
            if s == 0 and j == chunks // 2:
                keep_own().wait()
                near_all().wait()
                lax.fori_loop(1, groups // 2, begin(far_copy), 0)
        if s == 0:
            advance(len(queue))
    for j in range(chunks):
        fetch_back(j).wait()
    halves = cut(2)
    steps = [(s, span) for s in range(slots) for span in halves]
    for number, (s, span) in enumerate(steps):
        contract(s, span)
        if number > 0:
            settle(*steps[number - 1])
            if number % 2 == 0:
                put_rest(s - 1).start()
        if number == 2 * slots - 3:
            far_all().wait()
            lax.fori_loop(0, groups // 2, begin(twin_copy), 0)
    settle(*steps[-1])
    put_rest(slots - 1).start()
    twin_all().wait()
    for s in range(slots):
        put_rest(s).wait()


def run_finish(packet, states, context, stacks):
    (_, _, _, w_out, b_out, ln1_gain, ln1_bias, w_in, b_in, w_back, b_back, ln2_gain, ln2_bias) = (
        stacks
    )
    groups, lines = lax.axis_size("wide"), lax.axis_size("narrow")
    slots, length, width = context.shape
    units = w_in.shape[2]
    rows = length - LEAD
    place_hbm = pl.BlockSpec(memory_space=pl.ANY)
    vectors = (b_out, ln1_gain, ln1_bias, b_in, b_back, ln2_gain, ln2_bias)
    return pl.pallas_call(
        finish_kernel,
        name="finish",
        out_shape=(
            jax.ShapeDtypeStruct((groups, lines) + packet.shape, f32),
            jax.ShapeDtypeStruct((slots, rows, width), bf16),
        ),
        in_specs=[place_hbm] * 13,
        out_specs=(place_hbm, place_hbm),
        scratch_shapes=[
            pltpu.VMEM((slots, rows, width), bf16),
            pltpu.VMEM((slots, rows, width), bf16),
            pltpu.VMEM((width, width), bf16),
            pltpu.VMEM((width, units), bf16),
            pltpu.VMEM((units, width), bf16),
            pltpu.VMEM((slots, rows, width), f32),
            pltpu.VMEM((slots, rows, width), bf16),
            pltpu.VMEM((slots, rows, units), bf16),
            [pltpu.VMEM(vector.shape, f32) for vector in vectors],
            pltpu.SemaphoreType.DMA((2, slots)),
            pltpu.SemaphoreType.DMA((1 + 2 * (units // 512),)),
            pltpu.SemaphoreType.DMA((slots,)),
            pltpu.SemaphoreType.DMA((len(vectors),)),
        ]
        + [pltpu.SemaphoreType.DMA] * 7,
        compiler_params=pltpu.CompilerParams(
            collective_id=0,
            has_side_effects=True,
            vmem_limit_bytes=62 * 1024 * 1024,
        ),
    )(
        packet,
        states,
        context,
        w_out,
        w_in,
        w_back,
        *vectors,
    )


def ramps_kernel(
    gathered,
    states_in,
    rest,
    pool_w,
    pool_b,
    cls_w,
    cls_b,
    states,
    logits,
    losses,
    grad_pool_w,
    grad_pool_b,
    grad_cls_w,
    grad_cls_b,
    first_grads,
    all_buf,
    w_buf,
    g_buf,
    score_buf,
    inner_buf,
    rest_buf,
    in_bufs,
    out_bufs,
    w_sem,
    g_sem,
    s_sem,
    i_sem,
    r_sem,
):
    slots, depth, classes = logits.shape
    devices, packet, width = gathered.shape
    own = lax.axis_index("wide") * lax.axis_size("narrow") + lax.axis_index("narrow")

    def fetch(l):
        return pltpu.make_async_copy(pool_w.at[l], w_buf.at[l], w_sem.at[l])

    def put(l, t):
        span = pl.ds(t * 256, 256)
        return pltpu.make_async_copy(
            g_buf.at[l, span], grad_pool_w.at[l, span], g_sem.at[l, t]
        )

    def fetch_rest():
        return pltpu.make_async_copy(rest, rest_buf, s_sem.at[slots])

    def put_rest(s):
        return pltpu.make_async_copy(
            rest_buf.at[s], states.at[depth - 1, s, pl.ds(LEAD, rest.shape[1])], s_sem.at[s]
        )

    inputs = [
        pltpu.make_async_copy(source, target, i_sem.at[number])
        for number, (source, target) in enumerate(zip((pool_b, cls_w, cls_b), in_bufs))
    ]
    results = (logits, losses, grad_pool_b, grad_cls_w, grad_cls_b, first_grads)
    outputs = [
        pltpu.make_async_copy(source, target, r_sem.at[number])
        for number, (source, target) in enumerate(zip(out_bufs, results))
    ]
    pool_b, cls_w, cls_b = in_bufs
    logits, losses, grad_pool_b, grad_cls_w, grad_cls_b, first_grads = out_bufs
    gather_in = pltpu.make_async_copy(gathered, all_buf, s_sem.at[slots + 1])
    gather_in.start()
    for copy in inputs:
        copy.start()
    for l in range(depth):
        fetch(l).start()
    fetch_rest().start()
    gather_in.wait()
    for copy in inputs:
        copy.wait()

    unit = slots + 1
    rows = devices * unit
    pairs = all_buf[...].reshape(devices // 2, 2 * packet, width)
    even = pairs[:, :packet].reshape(rows, width)
    odd = pairs[:, packet:].reshape(rows, width)
    upper = lax.rem(lax.broadcasted_iota(jnp.int32, (rows, width), 0), packet) < unit
    firsts_all = (
        jnp.where(upper, even, pltpu.roll(odd, unit, 0)),
        jnp.where(upper, pltpu.roll(even, rows - unit, 0), odd),
    )
    place = lax.rem(lax.broadcasted_iota(jnp.int32, (rows, 128), 0), unit)
    marks = firsts_all[0][:, :128]
    spread = jnp.full((rows, 128), -1.0, f32)
    for s in range(slots):
        moved = pltpu.roll(marks, rows - (slots - s), 0)
        spread = jnp.where(place == s, moved[:, s : s + 1], spread)
    label_row = spread.T[:1]
    valid = (label_row >= 0).astype(f32)
    count = jnp.sum(valid)
    class_column = lax.broadcasted_iota(jnp.int32, (classes, rows), 0).astype(f32)
    onehot = (label_row == class_column).astype(f32)

    def mine(pair):
        return jnp.where(lax.rem(own, 2) == 0, pair[:slots], pair[unit : unit + slots])

    def dot(a, b):
        return jnp.dot(a, b, preferred_element_type=f32)

    def dot_turned(a, b):
        return lax.dot_general(a, b, (((1,), (1,)), ((), ())), preferred_element_type=f32)

    for l in range(depth):
        firsts_low = firsts_all[l].astype(bf16)
        firsts_turned = firsts_all[l].T.astype(bf16)
        cls = cls_w[:, l]
        cls_high, cls_low = split(cls)
        fetch(l).wait()
        weights, weights_low = split(w_buf[l])
        pooled = jnp.tanh(
            dot(firsts_low, weights) + dot(firsts_low, weights_low) + pool_b[l : l + 1]
        )
        pooled_high, pooled_low = split(pooled)
        scores = (
            dot_turned(cls_high, pooled_high)
            + (dot_turned(cls_low, pooled_high) + dot_turned(cls_high, pooled_low))
            + cls_b[l : l + 1].T
        )
        highest = jnp.max(scores, 0, keepdims=True)
        raised = jnp.exp(scores - highest)
        totals = jnp.sum(raised, 0, keepdims=True)
        grad = valid * (raised / totals - onehot) / count
        grad_column = grad.T
        inner = grad_column[:, 0:1] * cls[0:1]
        for c in range(1, classes):
            inner = inner + grad_column[:, c : c + 1] * cls[c : c + 1]
        inner = inner * (1.0 - pooled * pooled)
        inner_high, inner_low = split(inner)
        for t in range(width // 256):
            span = slice(t * 256, (t + 1) * 256)
            g_buf[l, span] = dot(firsts_turned[span], inner_high) + dot(
                firsts_turned[span], inner_low
            )
            put(l, t).start()
        grad_high, grad_low = split(grad)
        grad_cls_w[:, l] = dot(grad_high, pooled_high) + (
            dot(grad_low, pooled_high) + dot(grad_high, pooled_low)
        )
        inner_buf[...] = inner.reshape(devices // 2, packet, width)
        own_high, own_low = split(inner_buf[own // 2])
        own_grads = dot_turned(own_high, weights) + dot_turned(own_low, weights)
        first_grads[:, l] = mine(own_grads)
        grad_pool_b[l : l + 1] = jnp.sum(inner, 0, keepdims=True)
        grad_cls_b[l : l + 1] = jnp.sum(grad, 1, keepdims=True).T
        log_total = highest + jnp.log(totals)
        picked = jnp.sum(scores * onehot, 0, keepdims=True)
        losses[l] = jnp.sum(valid * (log_total - picked)) / count
        score_buf[...] = scores.T.reshape(devices // 2, packet, classes)
        logits[:, l] = mine(score_buf[own // 2])
        if l == 0:
            fetch_rest().wait()
            for s in range(slots):
                put_rest(s).start()
    for copy in outputs:
        copy.start()
    for l in range(depth):
        for t in range(width // 256):
            put(l, t).wait()
    for copy in outputs:
        copy.wait()
    for s in range(slots):
        put_rest(s).wait()


def run_ramps(gathered, states, rest, pool_w, pool_b, cls_w, cls_b):
    devices, packet, width = gathered.shape
    depth, classes = cls_b.shape
    slots = rest.shape[0]
    pairs = devices // 2
    place_hbm = pl.BlockSpec(memory_space=pl.ANY)
    cls_turned = jnp.transpose(cls_w, (2, 0, 1))
    states, logits, losses, pool_grad, pool_shift, cls_grad, cls_shift, first_grads = pl.pallas_call(
        ramps_kernel,
        name="ramps",
        out_shape=(
            jax.ShapeDtypeStruct(states.shape, states.dtype),
            jax.ShapeDtypeStruct((slots, depth, classes), f32),
            jax.ShapeDtypeStruct((depth,), f32),
            jax.ShapeDtypeStruct((depth, width, width), f32),
            jax.ShapeDtypeStruct((depth, width), f32),
            jax.ShapeDtypeStruct((classes, depth, width), f32),
            jax.ShapeDtypeStruct((depth, classes), f32),
            jax.ShapeDtypeStruct((slots, depth, width), f32),
        ),
        in_specs=[place_hbm] * 7,
        out_specs=(place_hbm,) * 8,
        input_output_aliases={1: 0},
        scratch_shapes=[
            pltpu.VMEM(gathered.shape, f32),
            pltpu.VMEM((depth, width, width), f32),
            pltpu.VMEM((depth, width, width), f32),
            pltpu.VMEM((pairs, packet, classes), f32),
            pltpu.VMEM((pairs, packet, width), f32),
            pltpu.VMEM(rest.shape, bf16),
            [pltpu.VMEM(member.shape, f32) for member in (pool_b, cls_turned, cls_b)],
            [
                pltpu.VMEM((slots, depth, classes), f32),
                pltpu.SMEM((depth,), f32),
                pltpu.VMEM((depth, width), f32),
                pltpu.VMEM((classes, depth, width), f32),
                pltpu.VMEM((depth, classes), f32),
                pltpu.VMEM((slots, depth, width), f32),
            ],
            pltpu.SemaphoreType.DMA((depth,)),
            pltpu.SemaphoreType.DMA((depth, width // 256)),
            pltpu.SemaphoreType.DMA((slots + 2,)),
            pltpu.SemaphoreType.DMA((3,)),
            pltpu.SemaphoreType.DMA((6,)),
        ],
        compiler_params=pltpu.CompilerParams(vmem_limit_bytes=62 * 1024 * 1024),
    )(gathered, states, rest, pool_w, pool_b, cls_turned, cls_b)
    return (
        states,
        jnp.transpose(logits, (1, 0, 2)),
        losses,
        pool_grad,
        pool_shift,
        jnp.transpose(cls_grad, (1, 2, 0)),
        cls_shift,
        jnp.transpose(first_grads, (1, 0, 2)),
    )


def local(
    hidden,
    lengths,
    slot_order,
    labels,
    w_qkv,
    b_query,
    b_value,
    w_out,
    b_out,
    ln1_gain,
    ln1_bias,
    w_in,
    b_in,
    w_back,
    b_back,
    ln2_gain,
    ln2_bias,
    pool_w,
    pool_b,
    cls_w,
    cls_b,
):
    stacks = (
        w_qkv,
        b_query,
        b_value,
        w_out,
        b_out,
        ln1_gain,
        ln1_bias,
        w_in,
        b_in,
        w_back,
        b_back,
        ln2_gain,
        ln2_bias,
    )
    states, context, packet = run_blocks(hidden, lengths, slot_order, labels, stacks)
    gathered, rest = run_finish(packet, states, context, stacks)
    gathered = gathered.reshape((-1,) + packet.shape)
    return run_ramps(gathered, states, rest, pool_w, pool_b, cls_w, cls_b)


def solution(mesh):
    both = ("wide", "narrow")
    return jax.shard_map(
        local,
        mesh=mesh,
        in_specs=(P(both, None, None), P(both), P(both), P(both)) + (P(),) * 17,
        out_specs=(
            P(None, both, None, None),
            P(None, both, None),
            P(),
            P(),
            P(),
            P(),
            P(),
            P(None, both, None),
        ),
        check_vma=False,
    )
```

profile of v0, /device:TPU:0, one launch (start us, length us, event | category | flops | bytes accessed | tf_op | source)
XLA Modules:
  0.0 87.1 jit_solution(7217940353978228734)
XLA Ops:
  0.6 54.6 %blocks.1 = (bf16[2,3,512,768]{3,2,1,0:T(8,128)(2,1)}, bf16[3,512,768]{2,1,0:T(8,128)(2,1)}, f32[8,768]{1,0:T(8,128)}) custom-call(s32[3]{0:T(128)} %order.1, s32[3]{0:T(128)} %lens.1, s32[3]{0:T(128)} %labels.1, bf16[3,512,768]{2,1,0:T(8,128)(2,1)} %hidden.1, bf16[2,768,2304]{2,1,0:T(8,128)(2,1)} %w_qkv.1, bf16[2,768,768]{2,1,0:T(8,128)(2,1)} %w_out.3, ...), custom_call_target="tpu_custom_call" | custom-call | tf_op jit(solution)/shard_map/blocks/pallas_call | solution.py:415
  55.2 23.0 %finish.1 = (f32[8,4,8,768]{3,2,1,0:T(8,128)}, bf16[3,384,768]{2,1,0:T(8,128)(2,1)}) custom-call(f32[8,768]{1,0:T(8,128)} %get-tuple-element.21.packet, bf16[2,3,512,768]{3,2,1,0:T(8,128)(2,1)} %get-tuple-element.22.states.states_in, bf16[3,512,768]{2,1,0:T(8,128)(2,1)} %get-tuple-element.23.context, bf16[2,768,768]{2,1,0:T(8,128)(2,1)} %w_out.3, ...), custom_call_target="tpu_custom_call" | custom-call | tf_op jit(solution)/shard_map/finish/pallas_call | solution.py:743
  78.2 8.6 %ramps.1 = (bf16[2,3,512,768]{3,2,1,0:T(8,128)(2,1)}, f32[3,2,3]{2,1,0:T(2,128)}, f32[2]{0:T(128)}, f32[2,768,768]{2,1,0:T(8,128)}, f32[2,768]{1,0:T(2,128)}, /*...) custom-call(f32[32,8,768]{2,1,0:T(8,128)} %bitcast.5, ...), custom_call_target="tpu_custom_call", output_to_operand_aliasing={{0}: (1, {})} | custom-call | tf_op jit(solution)/shard_map/ramps/pallas_call | solution.py:957
where the time goes:
time: 88.3 us; the launch traced here: 87.1 us
  Pallas kernels  86.2 us (98%)
  between operations  0.97 us (1%)
    pallas_call x1, Pallas kernels, run_blocks(): pl.pallas_call(blocks_kernel, name='blocks', out_shape=(jax.ShapeDtypeStr...  54.6 us
    pallas_call x1, Pallas kernels, run_finish(): pl.pallas_call(finish_kernel, name='finish', out_shape=(jax.ShapeDtypeStr...  23 us
    pallas_call x1, Pallas kernels, run_ramps(): pl.pallas_call(ramps_kernel, name='ramps', out_shape=(jax.ShapeDtypeStruc...  8.61 us

commit v1 on v0

--- a/solution.py
+++ b/solution.py
@@ -24,8 +24,8 @@
     return high, (values - high.astype(f32)).astype(bf16)
 
 
-def gelu(values):
-    return (0.5 * values) * (1.0 + lax.erf(values * math.sqrt(0.5)))
+def gelu_twice(values):
+    return values * (1.0 + lax.erf(values * math.sqrt(0.5)))
 
 
 def norm_rows(values, gain, shift):
@@ -139,8 +139,7 @@
         copy.start()
     q_buf[...] = jnp.zeros_like(q_buf)
     small[0].wait()
-    for number in range(slots):
-        fetch_x(number).start()
+    fetch_x(0).start()
     for copy in small[1:]:
         copy.wait()
 
@@ -242,10 +241,9 @@
                 fetch_x(s).wait()
 
             tiles = (lens[order[s]] + 127) // 128
-            for number in range(2, length // 128 + 1):
-                here = (tiles <= number) if number == 2 else (tiles == number)
-
-                @pl.when(here)
+            for number in range(1, length // 128 + 1):
+
+                @pl.when(tiles == number)
                 def _(number=number):
                     project(l, s, number * 128)
                     attend(s, number * 128)
@@ -276,11 +274,11 @@
         for j in range(hidden_units // chunk):
             units = slice(j * chunk, (j + 1) * chunk)
             inner = jnp.dot(mb_buf[slot, :size], in_buf[l, :, units], preferred_element_type=f32)
-            h_buf[slot, :size, units] = gelu(inner + b_in[l : l + 1, units]).astype(bf16)
+            h_buf[slot, :size, units] = gelu_twice(inner + b_in[l : l + 1, units]).astype(bf16)
 
     def contract(l, slot, size=tile):
         back = jnp.dot(h_buf[slot, :size], back_buf[l], preferred_element_type=f32)
-        y_buf[slot, :size] = m_buf[slot, :size] + back + b_back[l : l + 1]
+        y_buf[slot, :size] = m_buf[slot, :size] + 0.5 * back + b_back[l : l + 1]
 
     def settle(l, slot, size=tile):
         return norm_rows(y_buf[slot, :size], ln2_gain[l : l + 1], ln2_bias[l : l + 1]).astype(bf16)
@@ -335,6 +333,8 @@
         for j in range(width // 128):
             turn(0, part // 2 * (width // 128) + j)
     fetch_qkv(0, 1).wait()
+    for number in range(1, slots):
+        fetch_x(number).start()
 
     def layer(l, carry):
         for number in range(3):
@@ -669,11 +669,11 @@
     def expand(s, j):
         units = slice(j * chunk, (j + 1) * chunk)
         inner = jnp.dot(mb_buf[s], in_buf[:, units], preferred_element_type=f32)
-        h_buf[s, :, units] = gelu(inner + b_in[l : l + 1, units]).astype(bf16)
+        h_buf[s, :, units] = gelu_twice(inner + b_in[l : l + 1, units]).astype(bf16)
 
     def contract(s, span):
         back = jnp.dot(h_buf[s, span], back_buf[...], preferred_element_type=f32)
-        m_buf[s, span] = m_buf[s, span] + back + b_back[l : l + 1]
+        m_buf[s, span] = m_buf[s, span] + 0.5 * back + b_back[l : l + 1]
 
     def settle(s, span):
         x_buf[s, span] = norm_rows(
@@ -847,10 +847,11 @@
     gather_in.start()
     for copy in inputs:
         copy.start()
-    for l in range(depth):
+    fetch(0).start()
+    gather_in.wait()
+    for l in range(1, depth):
         fetch(l).start()
     fetch_rest().start()
-    gather_in.wait()
     for copy in inputs:
         copy.wait()
 
@@ -872,7 +873,7 @@
         spread = jnp.where(place == s, moved[:, s : s + 1], spread)
     label_row = spread.T[:1]
     valid = (label_row >= 0).astype(f32)
-    count = jnp.sum(valid)
+    count = jnp.sum(valid, 1, keepdims=True)
     class_column = lax.broadcasted_iota(jnp.int32, (classes, rows), 0).astype(f32)
     onehot = (label_row == class_column).astype(f32)
 
@@ -929,7 +930,7 @@
         grad_cls_b[l : l + 1] = jnp.sum(grad, 1, keepdims=True).T
         log_total = highest + jnp.log(totals)
         picked = jnp.sum(scores * onehot, 0, keepdims=True)
-        losses[l] = jnp.sum(valid * (log_total - picked)) / count
+        losses[l] = jnp.sum(valid * (log_total - picked) / count)
         score_buf[...] = scores.T.reshape(devices // 2, packet, classes)
         logits[:, l] = mine(score_buf[own // 2])
         if l == 0:

time: 88.3 us -> 88.2 us (level); the launches traced: 87.1 us -> 88.5 us
  Pallas kernels: 86.2 us -> 87.5 us
    pallas_call x1, Pallas kernels: 23 us -> 28.5 us  [run_finish(): pl.pallas_call(finish_kernel, name='finish', out_shape=(jax.ShapeDtypeStr...]
    pallas_call x1, Pallas kernels: 54.6 us -> 50.5 us  [run_blocks(): pl.pallas_call(blocks_kernel, name='blocks', out_shape=(jax.ShapeDtypeStr...]
where the time goes in v1:
time: 88.2 us; the launch traced here: 88.5 us
  Pallas kernels  87.5 us (99%)
  between operations  0.97 us (1%)
    pallas_call x1, Pallas kernels, run_blocks(): pl.pallas_call(blocks_kernel, name='blocks', out_shape=(jax.ShapeDtypeStr...  50.5 us
    pallas_call x1, Pallas kernels, run_finish(): pl.pallas_call(finish_kernel, name='finish', out_shape=(jax.ShapeDtypeStr...  28.5 us
    pallas_call x1, Pallas kernels, run_ramps(): pl.pallas_call(ramps_kernel, name='ramps', out_shape=(jax.ShapeDtypeStruc...  8.56 us

profile of v1, /device:TPU:0, one launch (start us, length us, event | category | flops | bytes accessed | tf_op | source)
XLA Modules:
  0.0 88.5 jit_solution(7018144927371801091)
XLA Ops:
  0.6 50.5 %blocks.1 = (bf16[2,3,512,768]{3,2,1,0:T(8,128)(2,1)}, bf16[3,512,768]{2,1,0:T(8,128)(2,1)}, f32[8,768]{1,0:T(8,128)}) custom-call(s32[3]{0:T(128)} %order.1, s32[3]{0:T(128)} %lens.1, s32[3]{0:T(128)} %labels.1, bf16[3,512,768]{2,1,0:T(8,128)(2,1)} %hidden.1, bf16[2,768,2304]{2,1,0:T(8,128)(2,1)} %w_qkv.1, bf16[2,768,768]{2,1,0:T(8,128)(2,1)} %w_out.3, ...), custom_call_target="tpu_custom_call" | custom-call | tf_op jit(solution)/shard_map/blocks/pallas_call | solution.py:415
  51.1 28.5 %finish.1 = (f32[8,4,8,768]{3,2,1,0:T(8,128)}, bf16[3,384,768]{2,1,0:T(8,128)(2,1)}) custom-call(f32[8,768]{1,0:T(8,128)} %get-tuple-element.21.packet, bf16[2,3,512,768]{3,2,1,0:T(8,128)(2,1)} %get-tuple-element.22.states.states_in, bf16[3,512,768]{2,1,0:T(8,128)(2,1)} %get-tuple-element.23.context, bf16[2,768,768]{2,1,0:T(8,128)(2,1)} %w_out.3, ...), custom_call_target="tpu_custom_call" | custom-call | tf_op jit(solution)/shard_map/finish/pallas_call | solution.py:743
  79.6 8.6 %ramps.1 = (bf16[2,3,512,768]{3,2,1,0:T(8,128)(2,1)}, f32[3,2,3]{2,1,0:T(2,128)}, f32[2]{0:T(128)}, f32[2,768,768]{2,1,0:T(8,128)}, f32[2,768]{1,0:T(2,128)}, /*...) custom-call(f32[32,8,768]{2,1,0:T(8,128)} %bitcast.5, ...), custom_call_target="tpu_custom_call", output_to_operand_aliasing={{0}: (1, {})} | custom-call | tf_op jit(solution)/shard_map/ramps/pallas_call | solution.py:958

commit v2 on v1

--- a/solution.py
+++ b/solution.py
@@ -622,13 +622,13 @@
             w_back.at[l, units], back_buf.at[units], w_sem.at[1 + chunks + j]
         )
 
-    def put_rest(s):
-        return pltpu.make_async_copy(x_buf.at[s], rest.at[s], o_sem.at[s])
+    def put_rest(s, span):
+        part = pl.ds(span.start, span.stop - span.start)
+        return pltpu.make_async_copy(
+            x_buf.at[s, part], rest.at[s, part], o_sem.at[s, span.start * 2 // rows]
+        )
 
     barrier = pltpu.get_barrier_semaphore()
-    lax.fori_loop(1, lines, greet(near), 0)
-    lax.fori_loop(1, groups // 2, greet(far), 0)
-    pl.semaphore_signal(barrier, inc=1, device_id=twin, device_id_type=MESH)
     vectors = (b_out, ln1_gain, ln1_bias, b_in, b_back, ln2_gain, ln2_bias)
     small = [
         pltpu.make_async_copy(source, target, v_sem.at[number])
@@ -647,9 +647,12 @@
         for _ in range(min(number, len(queue))):
             queue.pop().start()
 
+    advance(3)
     for copy in small:
         copy.start()
-    advance(3)
+    lax.fori_loop(1, lines, greet(near), 0)
+    lax.fori_loop(1, groups // 2, greet(far), 0)
+    pl.semaphore_signal(barrier, inc=1, device_id=twin, device_id_type=MESH)
     pl.semaphore_wait(barrier, lines + groups // 2 - 1)
     lax.fori_loop(1, lines, begin(near_copy), 0)
     keep_own().start()
@@ -718,16 +721,15 @@
         contract(s, span)
         if number > 0:
             settle(*steps[number - 1])
-            if number % 2 == 0:
-                put_rest(s - 1).start()
+            put_rest(*steps[number - 1]).start()
         if number == 2 * slots - 3:
             far_all().wait()
             lax.fori_loop(0, groups // 2, begin(twin_copy), 0)
     settle(*steps[-1])
-    put_rest(slots - 1).start()
+    put_rest(*steps[-1]).start()
     twin_all().wait()
-    for s in range(slots):
-        put_rest(s).wait()
+    for step in steps:
+        put_rest(*step).wait()
 
 
 def run_finish(packet, states, context, stacks):
@@ -761,7 +763,7 @@
             [pltpu.VMEM(vector.shape, f32) for vector in vectors],
             pltpu.SemaphoreType.DMA((2, slots)),
             pltpu.SemaphoreType.DMA((1 + 2 * (units // 512),)),
-            pltpu.SemaphoreType.DMA((slots,)),
+            pltpu.SemaphoreType.DMA((slots, 2)),
             pltpu.SemaphoreType.DMA((len(vectors),)),
         ]
         + [pltpu.SemaphoreType.DMA] * 7,

time: 88.2 us -> 89.5 us (1.015); the launches traced: 88.5 us -> 88.4 us
    pallas_call x1, Pallas kernels: 28.5 us -> 22.4 us  [run_finish(): pl.pallas_call(finish_kernel, name='finish', out_shape=(jax.ShapeDtypeStr...]
    pallas_call x1, Pallas kernels: 50.5 us -> 56.5 us  [run_blocks(): pl.pallas_call(blocks_kernel, name='blocks', out_shape=(jax.ShapeDtypeStr...]
where the time goes in v2:
time: 89.5 us; the launch traced here: 88.4 us
  Pallas kernels  87.4 us (98%)
  between operations  0.97 us (1%)
    pallas_call x1, Pallas kernels, run_blocks(): pl.pallas_call(blocks_kernel, name='blocks', out_shape=(jax.ShapeDtypeStr...  56.5 us
    pallas_call x1, Pallas kernels, run_finish(): pl.pallas_call(finish_kernel, name='finish', out_shape=(jax.ShapeDtypeStr...  22.4 us
    pallas_call x1, Pallas kernels, run_ramps(): pl.pallas_call(ramps_kernel, name='ramps', out_shape=(jax.ShapeDtypeStruc...  8.56 us

profile of v2, /device:TPU:0, one launch (start us, length us, event | category | flops | bytes accessed | tf_op | source)
XLA Modules:
  0.0 88.4 jit_solution(12576430303982531129)
XLA Ops:
  0.6 56.5 %blocks.1 = (bf16[2,3,512,768]{3,2,1,0:T(8,128)(2,1)}, bf16[3,512,768]{2,1,0:T(8,128)(2,1)}, f32[8,768]{1,0:T(8,128)}) custom-call(s32[3]{0:T(128)} %order.1, s32[3]{0:T(128)} %lens.1, s32[3]{0:T(128)} %labels.1, bf16[3,512,768]{2,1,0:T(8,128)(2,1)} %hidden.1, bf16[2,768,2304]{2,1,0:T(8,128)(2,1)} %w_qkv.1, bf16[2,768,768]{2,1,0:T(8,128)(2,1)} %w_out.3, ...), custom_call_target="tpu_custom_call" | custom-call | tf_op jit(solution)/shard_map/blocks/pallas_call | solution.py:415
  57.1 22.4 %finish.1 = (f32[8,4,8,768]{3,2,1,0:T(8,128)}, bf16[3,384,768]{2,1,0:T(8,128)(2,1)}) custom-call(f32[8,768]{1,0:T(8,128)} %get-tuple-element.21.packet, bf16[2,3,512,768]{3,2,1,0:T(8,128)(2,1)} %get-tuple-element.22.states.states_in, bf16[3,512,768]{2,1,0:T(8,128)(2,1)} %get-tuple-element.23.context, bf16[2,768,768]{2,1,0:T(8,128)(2,1)} %w_out.3, ...), custom_call_target="tpu_custom_call" | custom-call | tf_op jit(solution)/shard_map/finish/pallas_call | solution.py:745
  79.5 8.6 %ramps.1 = (bf16[2,3,512,768]{3,2,1,0:T(8,128)(2,1)}, f32[3,2,3]{2,1,0:T(2,128)}, f32[2]{0:T(128)}, f32[2,768,768]{2,1,0:T(8,128)}, f32[2,768]{1,0:T(2,128)}, /*...) custom-call(f32[32,8,768]{2,1,0:T(8,128)} %bitcast.5, ...), custom_call_target="tpu_custom_call", output_to_operand_aliasing={{0}: (1, {})} | custom-call | tf_op jit(solution)/shard_map/ramps/pallas_call | solution.py:960
